TPU v7x, 128 devices: a whole 4x4x4 slice. The times are simulated.
128 devices in a mesh: row: 8 (over x, core), col: 16 (over y, z).
Axes of the slice: x: 4, y: 4, z: 4, core: 2. Of those that a mesh axis runs over, the one named last changes fastest.
Arguments:
- phase: float32 [256, 256, 512], P(('row', 'col')), may hold values from -3.140625 to 3.140625
- dirty_map: float32 [256, 512], P(('row', 'col')), may hold values from 0.02 to 2
- pairs: int32 [3072, 2], P(('row', 'col')), may hold values from 0 to 255, as said below
- live: int32 [128], P(('row', 'col')), may hold values from 6 to 24, as said below
Outputs:
- solution: float32 [256, 512], P(('row', 'col'))
Inputs may be any that keep to these rules, and one draw needn't show every extreme that they name: Row k of pairs belongs to group g = k // 24 = i * 16 + j. Its first entry p satisfies (p // 2) // 16 == i, its second entry q satisfies (q // 2) % 16 == j, and q != p. Within one group, all first entries with the same p // 2 are equal, and all second entries with the same q // 2 are equal. Rows of a group at or after live[g] are ignored. `live`: some group has all 24 slots listed.
All inputs are finite; a program needn't handle non-finite values.
Results may differ from a plain program's by a relative error of at most 0.0043.
Values may be sent and summed in bfloat16 or wider, within the bound.
A program may use at most 128 MiB of HBM per device.

v0:
```python
import jax
import jax.numpy as jnp
from jax import lax
from jax.sharding import PartitionSpec as P

ITERS = 2


def psf_block(first_steer, second_steer, second_turned, mics):
    gram_real = jnp.dot(first_steer.T, second_steer, preferred_element_type=jnp.float32)
    gram_imag = jnp.dot(first_steer.T, second_turned, preferred_element_type=jnp.float32)
    scale = float(mics * mics - mics)
    return (gram_real * gram_real + gram_imag * gram_imag - float(mics)) / scale


def turn_steer(stacked, mics):
    return jnp.concatenate([stacked[:, mics:], -stacked[:, :mics]], axis=1)


def on_device(phase, dirty_map, pairs, live):
    col_count = lax.axis_size("col")
    tiles_here = phase.shape[0]
    mics = phase.shape[1]
    highest = lax.Precision.HIGHEST
    cosine = jnp.cos(phase).astype(jnp.bfloat16)
    sine_part = jnp.sin(phase).astype(jnp.bfloat16)
    stacked = jnp.concatenate([cosine, sine_part], axis=1)
    wide = stacked.astype(jnp.float32)
    power = jnp.sum(wide * wide, axis=1)
    diagonal = (power * power - float(mics)) / float(mics * mics - mics)
    own_turned = turn_steer(stacked, mics)
    count = live[0]
    first_owner = pairs[:, 0] // tiles_here % col_count
    second_owner = pairs[:, 1] // tiles_here // col_count
    first_offset = pairs[:, 0] % tiles_here
    second_offset = pairs[:, 1] % tiles_here
    row_steer = lax.all_gather(stacked, "col", axis=0, tiled=True)
    col_steer = lax.all_gather(stacked, "row", axis=0, tiled=True)
    first_steer_pos = first_owner * tiles_here + first_offset
    second_steer_pos = second_owner * tiles_here + second_offset
    col_turned = turn_steer(col_steer, mics)
    first_local = first_owner * tiles_here + first_offset
    second_local = second_owner * tiles_here + second_offset

    def listed_block(slot_index):
        first_pos = first_steer_pos[slot_index]
        second_pos = second_steer_pos[slot_index]
        first_steer = lax.dynamic_index_in_dim(row_steer, first_pos, 0, keepdims=False)
        second_steer = lax.dynamic_index_in_dim(col_steer, second_pos, 0, keepdims=False)
        second_turned = lax.dynamic_index_in_dim(col_turned, second_pos, 0, keepdims=False)
        return psf_block(first_steer, second_steer, second_turned, mics)

    def fetch_block(slot_index):
        return listed_block(slot_index)

    def own_block(tile_index):
        return psf_block(stacked[tile_index], stacked[tile_index], own_turned[tile_index], mics)

    def operator(estimate):
        map_first = lax.all_gather(estimate, "col", axis=0, tiled=True)
        map_second = lax.all_gather(estimate, "row", axis=0, tiled=True)

        def add_listed(slot_index, carry):
            first_sum, second_sum = carry
            first_pos = first_local[slot_index]
            second_pos = second_local[slot_index]
            block = fetch_block(slot_index)
            first_value = lax.dynamic_index_in_dim(map_first, first_pos, 0, keepdims=False)
            second_value = lax.dynamic_index_in_dim(map_second, second_pos, 0, keepdims=False)
            first_term = jnp.dot(block, second_value, precision=highest)
            second_term = jnp.dot(first_value, block, precision=highest)
            first_old = lax.dynamic_index_in_dim(first_sum, first_pos, 0, keepdims=False)
            second_old = lax.dynamic_index_in_dim(second_sum, second_pos, 0, keepdims=False)
            first_sum = lax.dynamic_update_index_in_dim(
                first_sum, first_old + first_term, first_pos, 0
            )
            second_sum = lax.dynamic_update_index_in_dim(
                second_sum, second_old + second_term, second_pos, 0
            )
            return (first_sum, second_sum)

        start_first = jnp.zeros(map_first.shape, jnp.float32)
        start_second = jnp.zeros(map_second.shape, jnp.float32)
        first_sum, second_sum = lax.fori_loop(0, count, add_listed, (start_first, start_second))
        own_terms = jnp.stack(
            [
                jnp.dot(own_block(tile_index), estimate[tile_index], precision=highest)
                for tile_index in range(tiles_here)
            ],
            axis=0,
        )
        first_part = lax.psum_scatter(first_sum, "col", scatter_dimension=0, tiled=True)
        second_part = lax.psum_scatter(second_sum, "row", scatter_dimension=0, tiled=True)
        shared = first_part + second_part
        return shared + own_terms

    estimate = jnp.maximum(dirty_map / diagonal, 0.0)
    for sweep in range(ITERS):
        estimate = jnp.maximum(estimate + (dirty_map - operator(estimate)) / diagonal, 0.0)
    return estimate


def solution(mesh):
    in_specs = (
        P(("row", "col"), None, None),
        P(("row", "col"), None),
        P(("row", "col"), None),
        P(("row", "col")),
    )
    out_specs = P(("row", "col"), None)
    return jax.shard_map(
        on_device, mesh=mesh, in_specs=in_specs, out_specs=out_specs, check_vma=False
    )
```

profile of v0, /device:TPU:1, one launch (start us, length us, event | category | flops | bytes accessed | tf_op | source)
XLA Modules:
  0.0 907.3 jit_solution(7599534553717347257)
XLA Ops:
  6.5 4.5 fusion.76
  11.0 4.4 sine_convert_fusion
  15.5 1.0 pad_maximum_fusion.1
  17.6 20.9 %all-gather.1 = f32[16,2,512]{2,1,0:T(2,128)S(1)} all-gather(f32[1,2,512]{2,1,0:T(2,128)S(1)} %bitcast.203), channel_id=1, replica_groups=mesh['row'=8,'col'=16] {'col'}, dimensions={0}, use_global_device_ids=true | all-gather | bytes 69632 | tf_op jit(solution)/shard_map/all_gather | solution.py:60
  38.5 18.7 %all-gather = f32[8,2,512]{2,1,0:T(2,128)S(1)} all-gather(f32[1,2,512]{2,1,0:T(2,128)S(1)} %bitcast.204), channel_id=1, replica_groups=mesh['row'=8,'col'=16] {'row'}, dimensions={0}, use_global_device_ids=true | all-gather | bytes 36864 | tf_op jit(solution)/shard_map/all_gather | solution.py:61
  60.2 9.9 %all-gather.9.cloned.1.call-done = bf16[16,512,512]{2,1,0:T(8,128)(2,1)} async-done(((bf16[2,512,512]{2,1,0:T(8,128)(2,1)}), bf16[16,512,512]{2,1,0:T(8,128)(2,1)}) %all-gather.9.cloned.1.call-update) | async-done | bytes 8388624 | tf_op jit(solution)/shard_map/all_gather | solution.py:38
  70.1 5.7 fusion.77
  75.8 7.8 pad_maximum_fusion
  83.6 99.9 %all-gather.7.cloned.1.call-done = bf16[32,512,512]{2,1,0:T(8,128)(2,1)} async-done(((bf16[2,512,512]{2,1,0:T(8,128)(2,1)}), bf16[32,512,512]{2,1,0:T(8,128)(2,1)}) %all-gather.7.cloned.1.call-update) | async-done | bytes 16777232 | tf_op jit(solution)/shard_map/all_gather | solution.py:37
  183.6 98.3 %while.30 = (s32[]{:T(128)}, f32[32,512]{1,0:T(8,128)S(1)}, f32[16,512]{1,0:T(8,128)S(1)}, s32[]{:T(128)}, s32[24]{0:T(128)S(1)}, /*index=5*/bf16[32,512,512]{2,...) while((s32[]{:T(128)}, f32[32,512]{1,0:T(8,128)S(1)}, ...), condition=%wide.region_2.3_spmd, body=%wide.region_1.2_spmd.sunk | while | flops 544474112 | bytes 7377211 | solution.py:84
  189.3 1.7 convolution_multiply_fusion.10
  190.9 1.7 fusion.116
  192.6 1.0 fusion.117
  200.1 1.7 convolution_multiply_fusion.10
  201.8 1.7 fusion.116
  210.9 1.7 convolution_multiply_fusion.10
  212.6 1.7 fusion.116
  214.3 1.0 fusion.117
  221.8 1.7 convolution_multiply_fusion.10
  223.5 1.7 fusion.116
  225.2 1.0 fusion.117
  232.6 1.7 convolution_multiply_fusion.10
  234.3 1.7 fusion.116
  236.0 1.0 fusion.117
  243.5 1.7 convolution_multiply_fusion.10
  245.2 1.7 fusion.116
  254.3 1.7 convolution_multiply_fusion.10
  256.0 1.7 fusion.116
  265.2 1.7 convolution_multiply_fusion.10
  266.9 1.7 fusion.116
  268.5 1.0 fusion.117
  276.0 1.7 convolution_multiply_fusion.10
  277.7 1.7 fusion.116
  279.4 1.0 fusion.117
  286.0 42.2 %all-reduce.1 = f32[16,512]{1,0:T(8,128)S(1)} all-reduce(f32[16,512]{1,0:T(8,128)S(1)} %get-tuple-element.356), channel_id=3, replica_groups=mesh['row'=8,'col'=16] {'row'}, use_global_device_ids=true, to_apply=%region_4.5.clone | all-reduce | flops 8192 | bytes 65536
  328.2 194.4 %all-reduce.7.cloned.1.call-done = f32[32,512]{1,0:T(8,128)} async-done(((f32[32,512]{1,0:T(8,128)}), f32[32,512]{1,0:T(8,128)}) %all-reduce.7.cloned.1.call-update) | async-done | bytes 65552
  523.4 17.5 %all-gather.3 = f32[16,2,512]{2,1,0:T(2,128)S(1)} all-gather(f32[1,2,512]{2,1,0:T(2,128)S(1)} %bitcast.205), channel_id=1, replica_groups=mesh['row'=8,'col'=16] {'col'}, dimensions={0}, use_global_device_ids=true | all-gather | bytes 69632 | tf_op jit(solution)/shard_map/all_gather | solution.py:60
  540.8 20.8 %all-gather.2 = f32[8,2,512]{2,1,0:T(2,128)S(1)} all-gather(f32[1,2,512]{2,1,0:T(2,128)S(1)} %bitcast.206), channel_id=1, replica_groups=mesh['row'=8,'col'=16] {'row'}, dimensions={0}, use_global_device_ids=true | all-gather | bytes 36864 | tf_op jit(solution)/shard_map/all_gather | solution.py:61
  562.8 98.4 %while.31 = (s32[]{:T(128)}, f32[32,512]{1,0:T(8,128)S(1)}, f32[16,512]{1,0:T(8,128)S(1)}, s32[]{:T(128)}, s32[24]{0:T(128)S(1)}, /*index=5*/bf16[32,512,512]{2,...) while((s32[]{:T(128)}, f32[32,512]{1,0:T(8,128)S(1)}, ...), condition=%wide.region_6.7_spmd, body=%wide.region_5.6_spmd.sunk | while | flops 544474112 | bytes 7377211 | solution.py:84
  568.5 1.7 convolution_multiply_fusion.11
  570.2 1.7 fusion.127
  579.3 1.7 convolution_multiply_fusion.11
  581.0 1.7 fusion.127
  590.2 1.7 convolution_multiply_fusion.11
  591.9 1.7 fusion.127
  601.1 1.7 convolution_multiply_fusion.11
  602.8 1.7 fusion.127
  611.9 1.7 convolution_multiply_fusion.11
  613.6 1.7 fusion.127
  622.8 1.7 convolution_multiply_fusion.11
  624.5 1.7 fusion.127
  626.2 1.0 fusion.128
  633.7 1.7 convolution_multiply_fusion.11
  635.3 1.7 fusion.127
  637.0 1.0 fusion.128
  644.5 1.7 convolution_multiply_fusion.11
  646.2 1.7 fusion.127
  647.9 1.0 fusion.128
  655.4 1.7 convolution_multiply_fusion.11
  657.1 1.7 fusion.127
  658.8 1.0 fusion.128
  662.8 41.4 %all-reduce.3 = f32[16,512]{1,0:T(8,128)S(1)} all-reduce(f32[16,512]{1,0:T(8,128)S(1)} %get-tuple-element.358), channel_id=5, replica_groups=mesh['row'=8,'col'=16] {'row'}, use_global_device_ids=true, to_apply=%region_8.9.clone | all-reduce | flops 8192 | bytes 65536
  704.2 195.3 %all-reduce.9.cloned.1.call-done = f32[32,512]{1,0:T(8,128)} async-done(((f32[32,512]{1,0:T(8,128)}), f32[32,512]{1,0:T(8,128)}) %all-reduce.9.cloned.1.call-update) | async-done | bytes 65552
  899.5 1.3 add_maximum_fusion
  (194 shorter events, 53.3 us)
Async XLA Ops:
  6.5 11.0 %copy-start.2 = (f32[2,512]{1,0:T(2,128)S(1)}, f32[2,512]{1,0:T(2,128)}, u32[]{:S(2)}) copy-start(f32[2,512]{1,0:T(2,128)} %param.9) | copy-start | bytes 12292
  6.5 51.7 %copy-start.3 = (s32[24,2]{0,1:T(2,128)S(1)}, s32[24,2]{0,1:T(2,128)}, u32[]{:S(2)}) copy-start(s32[24,2]{0,1:T(2,128)} %param.10) | copy-start | bytes 580
  6.5 63.6 %all-gather.9.cloned.1.call-start = ((), (), s32[]{:S(2)}) async-start(), calls=%async_computation.1 | async-start | bytes 9437184 | tf_op jit(solution)/shard_map/all_gather | solution.py:38
  16.5 167.0 %all-gather.7.cloned.1.call-start = ((), (), s32[]{:S(2)}) async-start(), calls=%async_computation | async-start | bytes 17825792 | tf_op jit(solution)/shard_map/all_gather | solution.py:37
  17.3 505.3 %all-reduce.7.cloned.1.call-start = ((), (), s32[]{:S(2)}) async-start(), calls=%async_computation.2 | async-start | bytes 131072
  183.5 100.0 %copy-start.5 = (u32[128]{0:T(128)S(1)}, u32[128]{0:T(128)}, u32[]{:S(2)}) copy-start(u32[128]{0:T(128)} %constant.215) | copy-start | bytes 1540
  183.5 100.6 %copy-start.4 = (u32[128]{0:T(128)S(1)}, u32[128]{0:T(128)}, u32[]{:S(2)}) copy-start(u32[128]{0:T(128)} %constant.219) | copy-start | bytes 1540
  281.8 0.6 copy-start.1
  282.5 617.0 %all-reduce.9.cloned.1.call-start = ((), (), s32[]{:S(2)}) async-start(), calls=%async_computation.3 | async-start | bytes 131072
  661.2 0.6 copy-start
Sparse Core Ops, SparseCore 0:
  16.7 53.4 all-gather.8
  72.3 111.1 all-gather.6
  282.6 239.9 all-reduce.6
  661.9 237.4 all-reduce.8
where the time goes:
time: 914 us; the launch traced here: 907 us
  waiting for transfers between devices  500 us (55%)
  blocking collectives  161 us (18%)
  matrix products  95 us (10%)
  loops' own time  83.5 us (9%)
  local copies, waits for them, and re-layouts  26.4 us (3%)
  other arithmetic  26 us (3%)
  between operations  14.6 us (2%)
    unnamed x6, waiting for transfers between devices  390 us
    all_gather x1, waiting for transfers between devices, on_device(): row_steer = lax.all_gather(stacked, 'col', axis=0, tiled=True)  99.9 us
    unnamed x2, blocking collectives  83.5 us
    another operation x2, loops' own time, operator(): lax.fori_loop(0, count, add_listed, (start_first, start_second))  83.5 us
    all_gather x2, blocking collectives, operator(): map_second = lax.all_gather(estimate, 'row', axis=0, tiled=True)  39.5 us
    all_gather x2, blocking collectives, operator(): map_first = lax.all_gather(estimate, 'col', axis=0, tiled=True)  38.3 us
    dot_general x20, matrix products, psf_block(): jnp.dot(first_steer.T, second_steer, preferred_element_type=jnp.float32)  31.2 us
    dot_general x20, matrix products, psf_block(): jnp.dot(first_steer.T, second_turned, preferred_element_type=jnp.float32)  31 us
  transfers between devices with their start and end apart: 4, of which 4 were waited for; matrix products, arithmetic and copies ran while one was open for 2% of the time, Pallas kernels for 0%

commit v1 on v0

v1 whole, which is shorter than its diff:
```python
import functools

import jax
import jax.numpy as jnp
from jax import lax
from jax.experimental import pallas as pl
from jax.experimental.pallas import tpu as pltpu
from jax.sharding import PartitionSpec as P

ITERS = 2
MESH = pl.DeviceIdType.MESH
BF = jnp.bfloat16
F32 = jnp.float32
COS = (1.0, -0.49999988079071045, 0.04166648909449577, -0.0013887806562706828,
       2.476993904565461e-05, -2.7079585152023355e-07, 1.7247135941644842e-09)
SIN = (1.0, -0.1666666567325592, 0.008333321660757065, -0.0001984053524211049,
       2.753588887571823e-06, -2.472918936291535e-08, 1.3614490090851916e-10)


def hops(offset):
    return sum(min(step, 4 - step) for step in offset)


OFFSETS = sorted(
    [(a, b, c) for a in range(4) for b in range(4) for c in range(4) if (a, b, c) != (0, 0, 0)],
    key=lambda offset: -hops(offset),
)


def polynomial(square, coefficients):
    total = jnp.full_like(square, coefficients[-1])
    for coefficient in coefficients[-2::-1]:
        total = total * square + coefficient
    return total


def dot(a, b):
    return jnp.dot(a, b, preferred_element_type=F32)


def dot_nt(a, b):
    return lax.dot_general(a, b, (((1,), (1,)), ((), ())), preferred_element_type=F32)


def kernel(
    phase_hbm, dirty_hbm, pairs_hbm, live_hbm, out_ref,
    phase, dirty, pairs, live, cos_b, sin_b, points, esum, ediff,
    send_h, own_h, other_h, send_s, got_s, flat, stack, work,
    rec_send, rec_got, sums_send, sums_got, count_send, count_got, count_f, count_b, eye_perm,
    load_sem, h_send, h_got, x_send, x_got, s_send, s_got, rec_ssem, rec_rsem, sum_ssem, sum_rsem,
    cnt_ssem, cnt_rsem,
):
    tiles, mics, width = phase.shape
    scale = float(mics * mics - mics)
    row, col = lax.axis_index("row"), lax.axis_index("col")
    x, core = lax.div(row, 2), lax.rem(row, 2)
    y, z = lax.div(col, 4), lax.rem(col, 4)
    me = col * 4 + x
    other = row + 1 - 2 * core

    loads = [
        pltpu.make_async_copy(phase_hbm.at[0], phase.at[0], load_sem.at[0]),
        pltpu.make_async_copy(phase_hbm.at[1], phase.at[1], load_sem.at[1]),
        pltpu.make_async_copy(dirty_hbm, dirty, load_sem.at[2]),
        pltpu.make_async_copy(pairs_hbm, pairs, load_sem.at[3]),
        pltpu.make_async_copy(live_hbm, live, load_sem.at[4]),
    ]
    for load in loads:
        load.start()

    barrier = pltpu.get_barrier_semaphore()
    for da, db, dc in OFFSETS:
        pl.semaphore_signal(
            barrier,
            inc=1,
            device_id=(lax.rem(x + da, 4) * 2 + core, lax.rem(y + db, 4) * 4 + lax.rem(z + dc, 4)),
            device_id_type=MESH,
        )
    for da in range(4):
        pl.semaphore_signal(
            barrier, inc=1, device_id=(lax.rem(x + da, 4) * 2 + 1 - core, col), device_id_type=MESH
        )

    lane = lax.broadcasted_iota(jnp.int32, (8, 128), 1)
    sub = lax.broadcasted_iota(jnp.int32, (8, 128), 0)
    chip_lane = col * 4 + x

    def sums_record(estimate):
        record = jnp.zeros((8, 128), F32)
        for t in range(tiles):
            total = jnp.sum(estimate[t : t + 1, :], axis=1, keepdims=True)
            record = jnp.where((sub == 4 + core) & (lane == t * 64 + chip_lane), total, record)
        return record

    def form(it, estimate):
        mats = []
        row_id = lax.broadcasted_iota(jnp.int32, (mics, mics), 0)
        col_id = lax.broadcasted_iota(jnp.int32, (mics, mics), 1)
        for t in range(tiles):
            value = estimate[t : t + 1, :]
            total = jnp.sum(value, axis=1, keepdims=True)
            left = jnp.concatenate(
                [(esum[t] * value).astype(BF), (ediff[t] * -value).astype(BF)], axis=1
            )
            mat = dot(left, points[t])
            mats.append(jnp.where(row_id == col_id, mat - total, mat))
        for half in range(2):
            parts = [m[:, half * 128 : half * 128 + 128].reshape(32, 8, 128) for m in mats]
            send_h[it, pl.ds(half * 32, 32)] = jnp.concatenate(parts, axis=1).astype(BF)

    def send_all(src, dst, ssem, rsem):
        for da, db, dc in OFFSETS:
            px = lax.rem(x + da, 4)
            pc = lax.rem(y + db, 4) * 4 + lax.rem(z + dc, 4)
            pltpu.make_async_remote_copy(
                src_ref=src.at[pc * 4 + px], dst_ref=dst.at[me], send_sem=ssem, recv_sem=rsem,
                device_id=(px * 2 + core, pc), device_id_type=MESH,
            ).start()

    def send_row(src, dst, ssem, rsem):
        for k in range(1, 8):
            pltpu.make_async_remote_copy(
                src_ref=src, dst_ref=dst.at[row], send_sem=ssem, recv_sem=rsem,
                device_id=(lax.rem(row + k, 8), col), device_id_type=MESH,
            ).start()

    def send_col(src, dst, ssem, rsem):
        for k in range(1, 16):
            pltpu.make_async_remote_copy(
                src_ref=src, dst_ref=dst, send_sem=ssem, recv_sem=rsem,
                device_id=(row, lax.rem(col + k, 16)), device_id_type=MESH,
            ).start()

    def wait(ref, sem):
        pltpu.make_async_copy(ref, ref, sem).wait()

    loads[2].wait()
    powers, diags, firsts = [], [], []
    for t in range(tiles):
        loads[t].wait()
        angle = phase[t]
        square = angle * angle
        cosine = polynomial(square, COS).astype(BF)
        sine = (polynomial(square, SIN) * angle).astype(BF)
        cos_b[t] = cosine
        sin_b[t] = sine
        cosine, sine = cosine.astype(F32), sine.astype(F32)
        esum[t] = cosine + sine
        ediff[t] = cosine - sine
        power = jnp.sum(cosine * cosine + sine * sine, axis=0, keepdims=True)
        diag = (power * power - float(mics)) / scale
        powers.append(power)
        diags.append(diag)
        firsts.append(jnp.maximum(dirty[t : t + 1, :] / diag, 0.0))
        points[t] = jnp.concatenate([cosine.T, sine.T], axis=0).astype(BF)
    power = jnp.concatenate(powers, axis=0)
    diag = jnp.concatenate(diags, axis=0)
    estimate = jnp.concatenate(firsts, axis=0)

    loads[3].wait()
    loads[4].wait()
    slots = pairs.shape[1]
    slot_id = lax.broadcasted_iota(jnp.int32, (slots, 128), 0)
    slot_lane = lax.broadcasted_iota(jnp.int32, (slots, 128), 1)
    place = (slot_lane == 32 * lax.rem(row, 4) + slot_id) & (slot_id < live[0])
    numbers = dot((pairs[...] + 1).astype(F32).astype(BF), place.astype(F32).astype(BF))
    half_id = lax.div(row, 4)
    record = sums_record(estimate)
    record = jnp.where(sub == half_id, numbers[0:1, :], record)
    record = jnp.where(sub == 2 + half_id, numbers[1:2, :], record)
    rec_send[0] = record
    rec_got[0, row] = record
    form(0, estimate)
    own_h[0, me] = send_h[0, me]

    raw = lax.broadcasted_iota(jnp.int32, (256, 256), 1)
    raw_row = (raw >> 1) & 7
    placed = (((raw_row + core) & 1) << 7) + ((raw & 1) << 6) + ((raw >> 4) << 2) + (raw_row >> 1)
    eye_perm[...] = (lax.broadcasted_iota(jnp.int32, (256, 256), 0) == placed).astype(F32).astype(BF)

    pl.semaphore_wait(barrier, len(OFFSETS) + 4)

    for it in range(ITERS):
        if it == 0:
            send_row(rec_send.at[0], rec_got.at[0], rec_ssem.at[0], rec_rsem.at[0])
        send_all(send_h.at[it], own_h.at[it], h_send.at[it], h_got.at[it])
        if it:
            send_row(rec_send.at[it], rec_got.at[it], rec_ssem.at[it], rec_rsem.at[it])
        else:
            wait(rec_got.at[0, pl.ds(0, 7)], rec_rsem.at[0])
            record = jnp.sum(rec_got[0], axis=0)
            sums_send[0] = record
            sums_got[0, col] = record
            counts = jnp.zeros((16, 256), F32)
            for half in range(2):
                first = record[half : half + 1, :].astype(jnp.int32) - 1
                second = record[2 + half : 3 + half, :].astype(jnp.int32) - 1
                first_pos = (
                    (((first >> 5) + core) & 1) * 128 + (first & 1) * 64
                    + ((first >> 1) & 15) * 4 + (first >> 6)
                )
                first_pos = jnp.where(first < 0, -1, first_pos)
                second_pos = jnp.where(second < 0, -1, (second >> 5) * 2 + (second & 1))
                first_hot = lax.broadcasted_iota(jnp.int32, (256, 128), 0) == first_pos
                second_hot = lax.broadcasted_iota(jnp.int32, (16, 128), 0) == second_pos
                counts = counts + dot_nt(
                    second_hot.astype(F32).astype(BF), first_hot.astype(F32).astype(BF)
                )
            count_send[...] = counts.astype(BF)
            here = pl.ds(pl.multiple_of(col * 16, 16), 16)
            count_got[here, :] = count_send[...]
            send_col(count_send, count_got.at[here], cnt_ssem, cnt_rsem)
            send_col(sums_send.at[0], sums_got.at[0, col], sum_ssem.at[0], sum_rsem.at[0])

        wait(own_h.at[it, pl.ds(0, 63)], h_got.at[it])
        exchange = pltpu.make_async_remote_copy(
            src_ref=own_h.at[it], dst_ref=other_h.at[it], send_sem=x_send.at[it],
            recv_sem=x_got.at[it], device_id=(other, col), device_id_type=MESH,
        )
        exchange.start()

        def stacked(source, base):
            flat[...] = source.astype(F32).reshape(1024, 128)
            for k in range(16):
                stack[base + (k // 8) * 64 : base + (k // 8) * 64 + 64,
                      (k % 8) * 128 : (k % 8) * 128 + 128] = flat[pl.ds(k, 64, stride=16), :].astype(BF)

        stacked(own_h[it], 0)
        if it == 0:
            wait(count_got.at[pl.ds(0, 240)], cnt_rsem)
            ordered = dot(eye_perm[...], count_got[...])
            here_id = lax.broadcasted_iota(jnp.int32, (128, 256), 0)
            all_id = lax.broadcasted_iota(jnp.int32, (128, 256), 1)
            counts = ordered[0:128, :] + ordered[:, 0:128].T + (here_id == all_id).astype(F32)
            count_f[...] = counts
            count_b[...] = counts.astype(BF)
        work[...] = dot(count_b[:, 0:128], stack[0:128, :])
        exchange.wait_recv()
        stacked(other_h[it], 128)
        total = work[...] + dot(count_b[:, 128:256], stack[128:256, :])
        for k in range(16):
            flat[pl.ds(k, 64, stride=16), :] = total[
                (k // 8) * 64 : (k // 8) * 64 + 64, (k % 8) * 128 : (k % 8) * 128 + 128
            ]
        send_s[it] = flat[...].reshape(64, 16, 128).astype(BF)
        got_s[it, me] = send_s[it, me]
        send_all(send_s.at[it], got_s.at[it], s_send.at[it], s_got.at[it])

        if it:
            wait(rec_got.at[it, pl.ds(0, 7)], rec_rsem.at[it])
            record = jnp.sum(rec_got[it], axis=0)
            sums_send[it] = record
            sums_got[it, col] = record
            send_col(sums_send.at[it], sums_got.at[it, col], sum_ssem.at[it], sum_rsem.at[it])
        wait(sums_got.at[it, pl.ds(0, 15)], sum_rsem.at[it])
        sums = jnp.sum(sums_got[it], axis=0)
        own_sums = jnp.where(core == 0, sums[4:5, :], sums[5:6, :])
        other_sums = jnp.where(core == 0, sums[5:6, :], sums[4:5, :])
        partner = jnp.concatenate([own_sums, other_sums], axis=1)
        spread = [
            jnp.sum(count_f[pl.ds(t * 64 + chip_lane, 1), :] * partner, axis=1, keepdims=True)
            for t in range(tiles)
        ]

        wait(got_s.at[it, pl.ds(0, 63)], s_got.at[it])
        news = []
        for t in range(tiles):
            mat = jnp.concatenate(
                [
                    got_s[it, half * 32 : half * 32 + 32].astype(F32)[:, t * 8 : t * 8 + 8, :].reshape(256, 128)
                    for half in range(2)
                ],
                axis=1,
            ).astype(BF)
            form_sum = jnp.sum(
                esum[t] * dot(mat, cos_b[t]) - ediff[t] * dot(mat, sin_b[t]), axis=0, keepdims=True
            )
            value = (form_sum + spread[t] * (power[t : t + 1] - float(mics))) / scale
            old = estimate[t : t + 1]
            news.append(jnp.maximum(old + (dirty[t : t + 1, :] - value) / diag[t : t + 1], 0.0))
        estimate = jnp.concatenate(news, axis=0)
        if it + 1 < ITERS:
            record = sums_record(estimate)
            rec_send[it + 1] = record
            rec_got[it + 1, row] = record
            form(it + 1, estimate)
            own_h[it + 1, me] = send_h[it + 1, me]

    out_ref[...] = estimate
    for it in range(ITERS):
        wait(send_h.at[it, pl.ds(0, 63)], h_send.at[it])
        wait(other_h.at[it], x_send.at[it])
        wait(send_s.at[it, pl.ds(0, 63)], s_send.at[it])
        wait(rec_got.at[it, pl.ds(0, 7)], rec_ssem.at[it])
        wait(sums_got.at[it, pl.ds(0, 15)], sum_ssem.at[it])
    wait(count_got.at[pl.ds(0, 240)], cnt_ssem)


def on_device(phase, dirty_map, pairs, live):
    tiles, mics, width = phase.shape
    vmem, dma = pltpu.VMEM, pltpu.SemaphoreType.DMA
    blocks = vmem((ITERS, 64, 16, 128), BF)
    return pl.pallas_call(
        kernel,
        out_shape=jax.ShapeDtypeStruct(dirty_map.shape, F32),
        in_specs=[pl.BlockSpec(memory_space=pl.ANY)] * 4,
        out_specs=pl.BlockSpec(memory_space=pltpu.VMEM),
        scratch_shapes=[
            vmem((tiles, mics, width), F32),
            vmem((tiles, width), F32),
            vmem((2, pairs.shape[0]), jnp.int32),
            pltpu.SMEM((1,), jnp.int32),
            vmem((tiles, mics, width), BF),
            vmem((tiles, mics, width), BF),
            vmem((tiles, 2 * width, mics), BF),
            vmem((tiles, mics, width), F32),
            vmem((tiles, mics, width), F32),
            blocks, blocks, blocks, blocks, blocks,
            vmem((1024, 128), F32),
            vmem((256, 1024), BF),
            vmem((128, 1024), F32),
            vmem((ITERS, 8, 128), F32),
            vmem((ITERS, 8, 8, 128), F32),
            vmem((ITERS, 8, 128), F32),
            vmem((ITERS, 16, 8, 128), F32),
            vmem((16, 256), BF),
            vmem((256, 256), BF),
            vmem((128, 256), F32),
            vmem((128, 256), BF),
            vmem((256, 256), BF),
            dma((5,)),
            dma((ITERS,)), dma((ITERS,)), dma((ITERS,)), dma((ITERS,)), dma((ITERS,)), dma((ITERS,)),
            dma((ITERS,)), dma((ITERS,)), dma((ITERS,)), dma((ITERS,)),
            dma, dma,
        ],
        compiler_params=pltpu.CompilerParams(
            collective_id=0, has_side_effects=True, vmem_limit_bytes=48 << 20
        ),
    )(phase, dirty_map, pairs.T, live)


def solution(mesh):
    in_specs = (
        P(("row", "col"), None, None),
        P(("row", "col"), None),
        P(("row", "col"), None),
        P(("row", "col")),
    )
    out_specs = P(("row", "col"), None)
    return jax.shard_map(
        on_device, mesh=mesh, in_specs=in_specs, out_specs=out_specs, check_vma=False
    )
```

time: 914 us -> 46.6 us (0.05)
  waiting for transfers between devices: 500 us -> 0 us
  blocking collectives: 161 us -> 0 us
  matrix products: 95 us -> 0 us
  loops' own time: 83.5 us -> 0 us
  Pallas kernels: 0 us -> 42.6 us
  other arithmetic: 26 us -> 0 us
  local copies, waits for them, and re-layouts: 26.4 us -> 3.18 us
  between operations: 14.6 us -> 0.67 us
    unnamed x6 -> x0, waiting for transfers between devices: 390 us -> none
    all_gather x2 -> x0, waiting for transfers between devices: 110 us -> none  [the longest x1 99.9 us: on_device(): row_steer = lax.all_gather(stacked, 'col', axis=0, tiled=True)]
    dot_general x80 -> x0, matrix products: 95 us -> none  [the longest x20 31.2 us: psf_block(): jnp.dot(first_steer.T, second_steer, preferred_element_type=jnp.float32)]
    unnamed x2 -> x0, blocking collectives: 83.5 us -> none
    another operation x2 -> x0, loops' own time: 83.5 us -> none  [operator(): lax.fori_loop(0, count, add_listed, (start_first, start_second))]
    all_gather x4 -> x0, blocking collectives: 77.9 us -> none  [the longest x2 39.5 us: operator(): map_second = lax.all_gather(estimate, 'row', axis=0, tiled=True)]
    pallas_call x0 -> x1, Pallas kernels: none -> 42.6 us  [on_device(): pl.pallas_call(kernel, out_shape=jax.ShapeDtypeStruct(dirty_map.shape, F3...]
    dynamic_slice x54 -> x0, local copies, waits for them, and re-layouts: 22 us -> none  [the longest x18 10.8 us: listed_block(): second_pos = second_steer_pos[slot_index]]
  transfers between devices with their start and end apart: 4 -> 0, of which waited for: 4 -> 0; matrix products, arithmetic and copies ran while one was open for 2% -> 0% of each run, Pallas kernels for 0% -> 0%
where the time goes in v1:
time: 46.6 us; the launch traced here: 46.5 us
  Pallas kernels  42.6 us (91%)
  local copies, waits for them, and re-layouts  3.18 us (7%)
  between operations  0.67 us (1%)
    pallas_call x1, Pallas kernels, on_device(): pl.pallas_call(kernel, out_shape=jax.ShapeDtypeStruct(dirty_map.shape, F3...  42.6 us
    unnamed x7, local copies, waits for them, and re-layouts  3.18 us

profile of v1, /device:TPU:1, one launch (start us, length us, event | category | flops | bytes accessed | tf_op | source)
XLA Modules:
  0.0 46.5 jit_solution(6639094616628968710)
XLA Ops:
  0.7 0.0 copy-start.2
  0.7 0.7 %copy-done.2 = s32[24,2]{0,1:T(2,128)S(1)} copy-done((s32[24,2]{0,1:T(2,128)S(1)}, s32[24,2]{0,1:T(2,128)}, u32[]{:S(2)}) %copy-start.2) | copy-done | bytes 216
  1.3 0.0 copy-start
  1.3 1.2 %copy-done = f32[2,256,512]{2,1,0:T(8,128)S(1)} copy-done((f32[2,256,512]{2,1,0:T(8,128)S(1)}, f32[2,256,512]{2,1,0:T(8,128)}, u32[]{:S(2)}) %copy-start) | copy-done | bytes 1048600
  2.6 0.0 copy-start.1
  2.6 0.7 %copy-done.1 = f32[2,512]{1,0:T(2,128)S(1)} copy-done((f32[2,512]{1,0:T(2,128)S(1)}, f32[2,512]{1,0:T(2,128)}, u32[]{:S(2)}) %copy-start.1) | copy-done | bytes 4120
  3.2 42.6 %shard_map.46 = f32[2,512]{1,0:T(2,128)S(1)} custom-call(f32[2,256,512]{2,1,0:T(8,128)S(1)} %copy-done, f32[2,512]{1,0:T(2,128)S(1)} %copy-done.1, s32[2,24]{1,0:T(2,128)S(1)} %bitcast.1, s32[1]{0:T(128)S(6)} %copy.6.live_hbm), custom_call_target="tpu_custom_call" | custom-call | tf_op jit(solution)/shard_map/pallas_call | solution.py:303
  45.9 0.6 %copy.7 = f32[2,512]{1,0:T(2,128)} copy(f32[2,512]{1,0:T(2,128)S(1)} %shard_map.46) | data formatting | bytes 8192
Async XLA Ops:
  0.7 0.7 %copy-start.2 = (s32[24,2]{0,1:T(2,128)S(1)}, s32[24,2]{0,1:T(2,128)}, u32[]{:S(2)}) copy-start(s32[24,2]{0,1:T(2,128)} %param.6) | copy-start | bytes 580
  1.3 1.2 %copy-start = (f32[2,256,512]{2,1,0:T(8,128)S(1)}, f32[2,256,512]{2,1,0:T(8,128)}, u32[]{:S(2)}) copy-start(f32[2,256,512]{2,1,0:T(8,128)} %phase_hbm.1) | copy-start | bytes 3145732
  2.6 0.7 %copy-start.1 = (f32[2,512]{1,0:T(2,128)S(1)}, f32[2,512]{1,0:T(2,128)}, u32[]{:S(2)}) copy-start(f32[2,512]{1,0:T(2,128)} %dirty_hbm.1) | copy-start | bytes 12292

commit v2 on v1

--- a/solution.py
+++ b/solution.py
@@ -46,9 +46,10 @@
     phase_hbm, dirty_hbm, pairs_hbm, live_hbm, out_ref,
     phase, dirty, pairs, live, cos_b, sin_b, points, esum, ediff,
     send_h, own_h, other_h, send_s, got_s, flat, stack, work,
-    rec_send, rec_got, sums_send, sums_got, count_send, count_got, count_f, count_b, eye_perm,
+    rec_send, rec_got, sums_send, sums_got, part_send, part_got, count_send, count_got, count_f, count_b,
+    eye_perm,
     load_sem, h_send, h_got, x_send, x_got, s_send, s_got, rec_ssem, rec_rsem, sum_ssem, sum_rsem,
-    cnt_ssem, cnt_rsem,
+    part_ssem, part_rsem, cnt_ssem, cnt_rsem,
 ):
     tiles, mics, width = phase.shape
     scale = float(mics * mics - mics)
@@ -118,18 +119,19 @@
             ).start()
 
     def send_row(src, dst, ssem, rsem):
-        for k in range(1, 8):
+        for k in (4, 5, 3, 2, 6, 7, 1):
             pltpu.make_async_remote_copy(
                 src_ref=src, dst_ref=dst.at[row], send_sem=ssem, recv_sem=rsem,
                 device_id=(lax.rem(row + k, 8), col), device_id_type=MESH,
             ).start()
 
     def send_col(src, dst, ssem, rsem):
-        for k in range(1, 16):
-            pltpu.make_async_remote_copy(
-                src_ref=src, dst_ref=dst, send_sem=ssem, recv_sem=rsem,
-                device_id=(row, lax.rem(col + k, 16)), device_id_type=MESH,
-            ).start()
+        for da, db, dc in OFFSETS:
+            if da == 0:
+                pltpu.make_async_remote_copy(
+                    src_ref=src, dst_ref=dst, send_sem=ssem, recv_sem=rsem,
+                    device_id=(row, lax.rem(y + db, 4) * 4 + lax.rem(z + dc, 4)), device_id_type=MESH,
+                ).start()
 
     def wait(ref, sem):
         pltpu.make_async_copy(ref, ref, sem).wait()
@@ -160,18 +162,20 @@
     loads[3].wait()
     loads[4].wait()
     slots = pairs.shape[1]
-    slot_id = lax.broadcasted_iota(jnp.int32, (slots, 128), 0)
-    slot_lane = lax.broadcasted_iota(jnp.int32, (slots, 128), 1)
-    place = (slot_lane == 32 * lax.rem(row, 4) + slot_id) & (slot_id < live[0])
-    numbers = dot((pairs[...] + 1).astype(F32).astype(BF), place.astype(F32).astype(BF))
-    half_id = lax.div(row, 4)
+    first, second = pairs[0:1, :], pairs[1:2, :]
+    first_lane = (first & 1) * 64 + ((first >> 1) & 15) * 4 + (first >> 6)
+    second_row = (second >> 5) * 2 + (second & 1)
+    listed = lax.broadcasted_iota(jnp.int32, (128, slots), 1) < live[0]
+    first_hot = (lax.broadcasted_iota(jnp.int32, (128, slots), 0) == first_lane) & listed
+    second_hot = lax.broadcasted_iota(jnp.int32, (16, slots), 0) == second_row
+    part_send[...] = dot_nt(
+        second_hot.astype(F32).astype(BF), first_hot.astype(F32).astype(BF)
+    ).astype(BF)
+    part_got[row] = part_send[...]
     record = sums_record(estimate)
-    record = jnp.where(sub == half_id, numbers[0:1, :], record)
-    record = jnp.where(sub == 2 + half_id, numbers[1:2, :], record)
     rec_send[0] = record
     rec_got[0, row] = record
     form(0, estimate)
-    own_h[0, me] = send_h[0, me]
 
     raw = lax.broadcasted_iota(jnp.int32, (256, 256), 1)
     raw_row = (raw >> 1) & 7
@@ -182,35 +186,20 @@
 
     for it in range(ITERS):
         if it == 0:
-            send_row(rec_send.at[0], rec_got.at[0], rec_ssem.at[0], rec_rsem.at[0])
+            send_row(part_send, part_got, part_ssem, part_rsem)
         send_all(send_h.at[it], own_h.at[it], h_send.at[it], h_got.at[it])
-        if it:
-            send_row(rec_send.at[it], rec_got.at[it], rec_ssem.at[it], rec_rsem.at[it])
-        else:
-            wait(rec_got.at[0, pl.ds(0, 7)], rec_rsem.at[0])
-            record = jnp.sum(rec_got[0], axis=0)
-            sums_send[0] = record
-            sums_got[0, col] = record
-            counts = jnp.zeros((16, 256), F32)
-            for half in range(2):
-                first = record[half : half + 1, :].astype(jnp.int32) - 1
-                second = record[2 + half : 3 + half, :].astype(jnp.int32) - 1
-                first_pos = (
-                    (((first >> 5) + core) & 1) * 128 + (first & 1) * 64
-                    + ((first >> 1) & 15) * 4 + (first >> 6)
-                )
-                first_pos = jnp.where(first < 0, -1, first_pos)
-                second_pos = jnp.where(second < 0, -1, (second >> 5) * 2 + (second & 1))
-                first_hot = lax.broadcasted_iota(jnp.int32, (256, 128), 0) == first_pos
-                second_hot = lax.broadcasted_iota(jnp.int32, (16, 128), 0) == second_pos
-                counts = counts + dot_nt(
-                    second_hot.astype(F32).astype(BF), first_hot.astype(F32).astype(BF)
-                )
-            count_send[...] = counts.astype(BF)
+        send_row(rec_send.at[it], rec_got.at[it], rec_ssem.at[it], rec_rsem.at[it])
+        own_h[it, me] = send_h[it, me]
+        if it == 0:
+            wait(part_got.at[pl.ds(0, 7)], part_rsem)
+            by_core = [
+                sum(part_got[2 * k + c].astype(F32) for k in range(4)).astype(BF) for c in range(2)
+            ]
+            count_send[:, 0:128] = jnp.where(core == 0, by_core[0], by_core[1])
+            count_send[:, 128:256] = jnp.where(core == 0, by_core[1], by_core[0])
             here = pl.ds(pl.multiple_of(col * 16, 16), 16)
             count_got[here, :] = count_send[...]
             send_col(count_send, count_got.at[here], cnt_ssem, cnt_rsem)
-            send_col(sums_send.at[0], sums_got.at[0, col], sum_ssem.at[0], sum_rsem.at[0])
 
         wait(own_h.at[it, pl.ds(0, 63)], h_got.at[it])
         exchange = pltpu.make_async_remote_copy(
@@ -218,12 +207,17 @@
             recv_sem=x_got.at[it], device_id=(other, col), device_id_type=MESH,
         )
         exchange.start()
+        wait(rec_got.at[it, pl.ds(0, 7)], rec_rsem.at[it])
+        record = jnp.sum(rec_got[it], axis=0)
+        sums_send[it] = record
+        sums_got[it, col] = record
+        send_col(sums_send.at[it], sums_got.at[it, col], sum_ssem.at[it], sum_rsem.at[it])
 
         def stacked(source, base):
-            flat[...] = source.astype(F32).reshape(1024, 128)
+            turned = jnp.swapaxes(source, 0, 1)
             for k in range(16):
                 stack[base + (k // 8) * 64 : base + (k // 8) * 64 + 64,
-                      (k % 8) * 128 : (k % 8) * 128 + 128] = flat[pl.ds(k, 64, stride=16), :].astype(BF)
+                      (k % 8) * 128 : (k % 8) * 128 + 128] = turned[k]
 
         stacked(own_h[it], 0)
         if it == 0:
@@ -238,20 +232,13 @@
         exchange.wait_recv()
         stacked(other_h[it], 128)
         total = work[...] + dot(count_b[:, 128:256], stack[128:256, :])
-        for k in range(16):
-            flat[pl.ds(k, 64, stride=16), :] = total[
-                (k // 8) * 64 : (k // 8) * 64 + 64, (k % 8) * 128 : (k % 8) * 128 + 128
-            ]
-        send_s[it] = flat[...].reshape(64, 16, 128).astype(BF)
+        cut = [
+            total[(k // 8) * 64 : (k // 8) * 64 + 64, (k % 8) * 128 : (k % 8) * 128 + 128]
+            for k in range(16)
+        ]
+        send_s[it] = jnp.swapaxes(jnp.stack(cut, axis=0), 0, 1).astype(BF)
+        send_all(send_s.at[it], got_s.at[it], s_send.at[it], s_got.at[it])
         got_s[it, me] = send_s[it, me]
-        send_all(send_s.at[it], got_s.at[it], s_send.at[it], s_got.at[it])
-
-        if it:
-            wait(rec_got.at[it, pl.ds(0, 7)], rec_rsem.at[it])
-            record = jnp.sum(rec_got[it], axis=0)
-            sums_send[it] = record
-            sums_got[it, col] = record
-            send_col(sums_send.at[it], sums_got.at[it, col], sum_ssem.at[it], sum_rsem.at[it])
         wait(sums_got.at[it, pl.ds(0, 15)], sum_rsem.at[it])
         sums = jnp.sum(sums_got[it], axis=0)
         own_sums = jnp.where(core == 0, sums[4:5, :], sums[5:6, :])
@@ -284,7 +271,6 @@
             rec_send[it + 1] = record
             rec_got[it + 1, row] = record
             form(it + 1, estimate)
-            own_h[it + 1, me] = send_h[it + 1, me]
 
     out_ref[...] = estimate
     for it in range(ITERS):
@@ -294,6 +280,7 @@
         wait(rec_got.at[it, pl.ds(0, 7)], rec_ssem.at[it])
         wait(sums_got.at[it, pl.ds(0, 15)], sum_ssem.at[it])
     wait(count_got.at[pl.ds(0, 240)], cnt_ssem)
+    wait(part_got.at[pl.ds(0, 7)], part_ssem)
 
 
 def on_device(phase, dirty_map, pairs, live):
@@ -323,6 +310,8 @@
             vmem((ITERS, 8, 8, 128), F32),
             vmem((ITERS, 8, 128), F32),
             vmem((ITERS, 16, 8, 128), F32),
+            vmem((16, 128), BF),
+            vmem((8, 16, 128), BF),
             vmem((16, 256), BF),
             vmem((256, 256), BF),
             vmem((128, 256), F32),
@@ -331,12 +320,12 @@
             dma((5,)),
             dma((ITERS,)), dma((ITERS,)), dma((ITERS,)), dma((ITERS,)), dma((ITERS,)), dma((ITERS,)),
             dma((ITERS,)), dma((ITERS,)), dma((ITERS,)), dma((ITERS,)),
-            dma, dma,
+            dma, dma, dma, dma,
         ],
         compiler_params=pltpu.CompilerParams(
             collective_id=0, has_side_effects=True, vmem_limit_bytes=48 << 20
         ),
-    )(phase, dirty_map, pairs.T, live)
+    )(*[pltpu.with_memory_space_constraint(v, pltpu.HBM) for v in (phase, dirty_map, pairs.T)], live)
 
 
 def solution(mesh):

time: 46.6 us -> 43.2 us (0.927)
  local copies, waits for them, and re-layouts: 3.18 us -> 0.6 us
  Pallas kernels: 42.6 us -> 41.8 us
    unnamed x7 -> x1, local copies, waits for them, and re-layouts: 3.18 us -> 0.6 us
    pallas_call x1, Pallas kernels: 42.6 us -> 41.8 us  [on_device(): pl.pallas_call(kernel, out_shape=jax.ShapeDtypeStruct(dirty_map.shape, F3...]
where the time goes in v2:
time: 43.2 us; the launch traced here: 43.1 us
  Pallas kernels  41.8 us (97%)
  between operations  0.66 us (2%)
  local copies, waits for them, and re-layouts  0.6 us (1%)
    pallas_call x1, Pallas kernels, on_device(): pl.pallas_call(kernel, out_shape=jax.ShapeDtypeStruct(dirty_map.shape, F3...  41.8 us

profile of v2, /device:TPU:1, one launch (start us, length us, event | category | flops | bytes accessed | tf_op | source)
XLA Modules:
  0.0 43.1 jit_solution(8099418618166665670)
XLA Ops:
  0.7 41.8 %shard_map.46 = f32[2,512]{1,0:T(2,128)S(1)} custom-call(f32[2,256,512]{2,1,0:T(8,128)} %phase_hbm.1, f32[2,512]{1,0:T(2,128)} %dirty_hbm.1, s32[2,24]{1,0:T(2,128)} %bitcast.1, s32[1]{0:T(128)S(6)} %copy.6.live_hbm), custom_call_target="tpu_custom_call" | custom-call | tf_op jit(solution)/shard_map/pallas_call | solution.py:290
  42.5 0.6 %copy.7 = f32[2,512]{1,0:T(2,128)} copy(f32[2,512]{1,0:T(2,128)S(1)} %shard_map.46) | data formatting | bytes 8192

commit v3 on v2

--- a/solution.py
+++ b/solution.py
@@ -11,10 +11,10 @@
 MESH = pl.DeviceIdType.MESH
 BF = jnp.bfloat16
 F32 = jnp.float32
-COS = (1.0, -0.49999988079071045, 0.04166648909449577, -0.0013887806562706828,
-       2.476993904565461e-05, -2.7079585152023355e-07, 1.7247135941644842e-09)
-SIN = (1.0, -0.1666666567325592, 0.008333321660757065, -0.0001984053524211049,
-       2.753588887571823e-06, -2.472918936291535e-08, 1.3614490090851916e-10)
+HALF_COS = (0.9999999403953552, -0.1249997615814209, 0.002603973960503936, -2.1646421373588964e-05,
+            9.044592985674171e-08)
+HALF_SIN = (0.5, -0.020833322778344154, 0.0002604078617878258, -1.5475848158530425e-06,
+            5.0883919300304115e-09)
 
 
 def hops(offset):
@@ -59,6 +59,17 @@
     me = col * 4 + x
     other = row + 1 - 2 * core
 
+    barrier = pltpu.get_barrier_semaphore()
+
+    def greet(px, pc, pcore):
+        pl.semaphore_signal(
+            barrier, inc=1, device_id=(px * 2 + pcore, pc), device_id_type=MESH
+        )
+
+    for offset in OFFSETS[:22]:
+        px, pc = lax.rem(x + offset[0], 4), lax.rem(y + offset[1], 4) * 4 + lax.rem(z + offset[2], 4)
+        greet(px, pc, core)
+
     loads = [
         pltpu.make_async_copy(phase_hbm.at[0], phase.at[0], load_sem.at[0]),
         pltpu.make_async_copy(phase_hbm.at[1], phase.at[1], load_sem.at[1]),
@@ -69,18 +80,11 @@
     for load in loads:
         load.start()
 
-    barrier = pltpu.get_barrier_semaphore()
-    for da, db, dc in OFFSETS:
-        pl.semaphore_signal(
-            barrier,
-            inc=1,
-            device_id=(lax.rem(x + da, 4) * 2 + core, lax.rem(y + db, 4) * 4 + lax.rem(z + dc, 4)),
-            device_id_type=MESH,
-        )
+    for offset in OFFSETS[22:]:
+        px, pc = lax.rem(x + offset[0], 4), lax.rem(y + offset[1], 4) * 4 + lax.rem(z + offset[2], 4)
+        greet(px, pc, core)
     for da in range(4):
-        pl.semaphore_signal(
-            barrier, inc=1, device_id=(lax.rem(x + da, 4) * 2 + 1 - core, col), device_id_type=MESH
-        )
+        greet(lax.rem(x + da, 4), col, 1 - core)
 
     lane = lax.broadcasted_iota(jnp.int32, (8, 128), 1)
     sub = lax.broadcasted_iota(jnp.int32, (8, 128), 0)
@@ -142,8 +146,10 @@
         loads[t].wait()
         angle = phase[t]
         square = angle * angle
-        cosine = polynomial(square, COS).astype(BF)
-        sine = (polynomial(square, SIN) * angle).astype(BF)
+        half_sine = polynomial(square, HALF_SIN) * angle
+        twice = half_sine + half_sine
+        cosine = (1.0 - twice * half_sine).astype(BF)
+        sine = (twice * polynomial(square, HALF_COS)).astype(BF)
         cos_b[t] = cosine
         sin_b[t] = sine
         cosine, sine = cosine.astype(F32), sine.astype(F32)
@@ -188,7 +194,8 @@
         if it == 0:
             send_row(part_send, part_got, part_ssem, part_rsem)
         send_all(send_h.at[it], own_h.at[it], h_send.at[it], h_got.at[it])
-        send_row(rec_send.at[it], rec_got.at[it], rec_ssem.at[it], rec_rsem.at[it])
+        if it:
+            send_row(rec_send.at[it], rec_got.at[it], rec_ssem.at[it], rec_rsem.at[it])
         own_h[it, me] = send_h[it, me]
         if it == 0:
             wait(part_got.at[pl.ds(0, 7)], part_rsem)
@@ -200,6 +207,7 @@
             here = pl.ds(pl.multiple_of(col * 16, 16), 16)
             count_got[here, :] = count_send[...]
             send_col(count_send, count_got.at[here], cnt_ssem, cnt_rsem)
+            send_row(rec_send.at[it], rec_got.at[it], rec_ssem.at[it], rec_rsem.at[it])
 
         wait(own_h.at[it, pl.ds(0, 63)], h_got.at[it])
         exchange = pltpu.make_async_remote_copy(
@@ -220,7 +228,13 @@
                       (k % 8) * 128 : (k % 8) * 128 + 128] = turned[k]
 
         stacked(own_h[it], 0)
-        if it == 0:
+        if it:
+            work[...] = dot(count_b[:, 0:128], stack[0:128, :])
+        exchange.wait_recv()
+        stacked(other_h[it], 128)
+        if it:
+            total = work[...] + dot(count_b[:, 128:256], stack[128:256, :])
+        else:
             wait(count_got.at[pl.ds(0, 240)], cnt_rsem)
             ordered = dot(eye_perm[...], count_got[...])
             here_id = lax.broadcasted_iota(jnp.int32, (128, 256), 0)
@@ -228,10 +242,7 @@
             counts = ordered[0:128, :] + ordered[:, 0:128].T + (here_id == all_id).astype(F32)
             count_f[...] = counts
             count_b[...] = counts.astype(BF)
-        work[...] = dot(count_b[:, 0:128], stack[0:128, :])
-        exchange.wait_recv()
-        stacked(other_h[it], 128)
-        total = work[...] + dot(count_b[:, 128:256], stack[128:256, :])
+            total = dot(count_b[...], stack[...])
         cut = [
             total[(k // 8) * 64 : (k // 8) * 64 + 64, (k % 8) * 128 : (k % 8) * 128 + 128]
             for k in range(16)

time: 43.2 us -> 42.9 us (level)
  no operation moved by 1% of the time
where the time goes in v3:
time: 42.9 us; the launch traced here: 42.7 us
  Pallas kernels  41.5 us (97%)
  between operations  0.66 us (2%)
  local copies, waits for them, and re-layouts  0.6 us (1%)
    pallas_call x1, Pallas kernels, on_device(): pl.pallas_call(kernel, out_shape=jax.ShapeDtypeStruct(dirty_map.shape, F3...  41.5 us

profile of v3, /device:TPU:1, one launch (start us, length us, event | category | flops | bytes accessed | tf_op | source)
XLA Modules:
  0.0 42.7 jit_solution(15095411314597181082)
XLA Ops:
  0.7 41.5 %shard_map.46 = f32[2,512]{1,0:T(2,128)S(1)} custom-call(f32[2,256,512]{2,1,0:T(8,128)} %phase_hbm.1, f32[2,512]{1,0:T(2,128)} %dirty_hbm.1, s32[2,24]{1,0:T(2,128)} %bitcast.1, s32[1]{0:T(128)S(6)} %copy.6.live_hbm), custom_call_target="tpu_custom_call" | custom-call | tf_op jit(solution)/shard_map/pallas_call | solution.py:301
  42.1 0.6 %copy.7 = f32[2,512]{1,0:T(2,128)} copy(f32[2,512]{1,0:T(2,128)S(1)} %shard_map.46) | data formatting | bytes 8192

commit v4 on v3

--- a/solution.py
+++ b/solution.py
@@ -45,7 +45,7 @@
 def kernel(
     phase_hbm, dirty_hbm, pairs_hbm, live_hbm, out_ref,
     phase, dirty, pairs, live, cos_b, sin_b, points, esum, ediff,
-    send_h, own_h, other_h, send_s, got_s, flat, stack, work,
+    send_h, own_h, other_h, send_s, got_s, send_f, in_f, out_f, got_f, stack,
     rec_send, rec_got, sums_send, sums_got, part_send, part_got, count_send, count_got, count_f, count_b,
     eye_perm,
     load_sem, h_send, h_got, x_send, x_got, s_send, s_got, rec_ssem, rec_rsem, sum_ssem, sum_rsem,
@@ -97,7 +97,7 @@
             record = jnp.where((sub == 4 + core) & (lane == t * 64 + chip_lane), total, record)
         return record
 
-    def form(it, estimate):
+    def form(estimate):
         mats = []
         row_id = lax.broadcasted_iota(jnp.int32, (mics, mics), 0)
         col_id = lax.broadcasted_iota(jnp.int32, (mics, mics), 1)
@@ -109,9 +109,34 @@
             )
             mat = dot(left, points[t])
             mats.append(jnp.where(row_id == col_id, mat - total, mat))
+        return mats
+
+    upper = lax.broadcasted_iota(jnp.int32, (32, 8, 128), 1) < 4
+
+    def cut_by_chip(mats):
         for half in range(2):
             parts = [m[:, half * 128 : half * 128 + 128].reshape(32, 8, 128) for m in mats]
-            send_h[it, pl.ds(half * 32, 32)] = jnp.concatenate(parts, axis=1).astype(BF)
+            send_h[pl.ds(half * 32, 32)] = jnp.concatenate(parts, axis=1).astype(BF)
+
+    def cut_by_core(mats):
+        for half in range(2):
+            first, second = [m[:, half * 128 : half * 128 + 128].reshape(32, 8, 128) for m in mats]
+            second = pltpu.roll(second, 4, 1)
+            send_f[pl.ds(half * 32, 32), 0] = jnp.where(upper, first, second).astype(BF)
+            send_f[pl.ds(half * 32, 32), 1] = jnp.where(upper, second, first).astype(BF)
+
+    def send_each(src, dst, ssem, rsem):
+        for da, db, dc in OFFSETS + [(0, 0, 0)]:
+            px = lax.rem(x + da, 4)
+            pc = lax.rem(y + db, 4) * 4 + lax.rem(z + dc, 4)
+            for apart in range(2):
+                if (da, db, dc) != (0, 0, 0) or apart:
+                    pcore = 1 - core if apart else core
+                    pltpu.make_async_remote_copy(
+                        src_ref=src(pc * 4 + px, pcore, apart), dst_ref=dst(apart),
+                        send_sem=ssem, recv_sem=rsem,
+                        device_id=(px * 2 + pcore, pc), device_id_type=MESH,
+                    ).start()
 
     def send_all(src, dst, ssem, rsem):
         for da, db, dc in OFFSETS:
@@ -181,7 +206,7 @@
     record = sums_record(estimate)
     rec_send[0] = record
     rec_got[0, row] = record
-    form(0, estimate)
+    cut_by_chip(form(estimate))
 
     raw = lax.broadcasted_iota(jnp.int32, (256, 256), 1)
     raw_row = (raw >> 1) & 7
@@ -193,11 +218,8 @@
     for it in range(ITERS):
         if it == 0:
             send_row(part_send, part_got, part_ssem, part_rsem)
-        send_all(send_h.at[it], own_h.at[it], h_send.at[it], h_got.at[it])
-        if it:
-            send_row(rec_send.at[it], rec_got.at[it], rec_ssem.at[it], rec_rsem.at[it])
-        own_h[it, me] = send_h[it, me]
-        if it == 0:
+            send_all(send_h, own_h, h_send.at[0], h_got.at[0])
+            own_h[me] = send_h[me]
             wait(part_got.at[pl.ds(0, 7)], part_rsem)
             by_core = [
                 sum(part_got[2 * k + c].astype(F32) for k in range(4)).astype(BF) for c in range(2)
@@ -207,49 +229,79 @@
             here = pl.ds(pl.multiple_of(col * 16, 16), 16)
             count_got[here, :] = count_send[...]
             send_col(count_send, count_got.at[here], cnt_ssem, cnt_rsem)
+            send_row(rec_send.at[0], rec_got.at[0], rec_ssem.at[0], rec_rsem.at[0])
+            wait(own_h.at[pl.ds(0, 63)], h_got.at[0])
+            exchange = pltpu.make_async_remote_copy(
+                src_ref=own_h, dst_ref=other_h, send_sem=x_send, recv_sem=x_got,
+                device_id=(other, col), device_id_type=MESH,
+            )
+            exchange.start()
+        else:
+            send_each(
+                lambda slot, pcore, apart: send_f.at[slot, pcore],
+                lambda apart: in_f.at[apart * 64 + me],
+                h_send.at[it], h_got.at[it],
+            )
             send_row(rec_send.at[it], rec_got.at[it], rec_ssem.at[it], rec_rsem.at[it])
-
-        wait(own_h.at[it, pl.ds(0, 63)], h_got.at[it])
-        exchange = pltpu.make_async_remote_copy(
-            src_ref=own_h.at[it], dst_ref=other_h.at[it], send_sem=x_send.at[it],
-            recv_sem=x_got.at[it], device_id=(other, col), device_id_type=MESH,
-        )
-        exchange.start()
+            in_f[me] = send_f[me, core]
+
         wait(rec_got.at[it, pl.ds(0, 7)], rec_rsem.at[it])
         record = jnp.sum(rec_got[it], axis=0)
         sums_send[it] = record
         sums_got[it, col] = record
         send_col(sums_send.at[it], sums_got.at[it, col], sum_ssem.at[it], sum_rsem.at[it])
 
-        def stacked(source, base):
-            turned = jnp.swapaxes(source, 0, 1)
-            for k in range(16):
-                stack[base + (k // 8) * 64 : base + (k // 8) * 64 + 64,
-                      (k % 8) * 128 : (k % 8) * 128 + 128] = turned[k]
-
-        stacked(own_h[it], 0)
-        if it:
-            work[...] = dot(count_b[:, 0:128], stack[0:128, :])
-        exchange.wait_recv()
-        stacked(other_h[it], 128)
-        if it:
-            total = work[...] + dot(count_b[:, 128:256], stack[128:256, :])
-        else:
+        if it == 0:
+            for base, source in ((0, own_h), (128, other_h)):
+                if base:
+                    exchange.wait_recv()
+                turned = jnp.swapaxes(source[...], 0, 1)
+                for k in range(16):
+                    stack[base + (k // 8) * 64 : base + (k // 8) * 64 + 64,
+                          (k % 8) * 128 : (k % 8) * 128 + 128] = turned[k]
             wait(count_got.at[pl.ds(0, 240)], cnt_rsem)
             ordered = dot(eye_perm[...], count_got[...])
             here_id = lax.broadcasted_iota(jnp.int32, (128, 256), 0)
             all_id = lax.broadcasted_iota(jnp.int32, (128, 256), 1)
             counts = ordered[0:128, :] + ordered[:, 0:128].T + (here_id == all_id).astype(F32)
             count_f[...] = counts
-            count_b[...] = counts.astype(BF)
-            total = dot(count_b[...], stack[...])
-        cut = [
-            total[(k // 8) * 64 : (k // 8) * 64 + 64, (k % 8) * 128 : (k % 8) * 128 + 128]
-            for k in range(16)
-        ]
-        send_s[it] = jnp.swapaxes(jnp.stack(cut, axis=0), 0, 1).astype(BF)
-        send_all(send_s.at[it], got_s.at[it], s_send.at[it], s_got.at[it])
-        got_s[it, me] = send_s[it, me]
+            count_b[0:128, :] = counts.astype(BF)
+            total = dot(count_b[0:128, :], stack[...])
+            cut = [
+                total[(k // 8) * 64 : (k // 8) * 64 + 64, (k % 8) * 128 : (k % 8) * 128 + 128]
+                for k in range(16)
+            ]
+            send_s[...] = jnp.swapaxes(jnp.stack(cut, axis=0), 0, 1).astype(BF)
+            send_all(send_s, got_s, s_send.at[0], s_got.at[0])
+            got_s[me] = send_s[me]
+            counts = ordered[128:256, :] + ordered[:, 128:256].T + (here_id + 128 == all_id).astype(F32)
+            count_b[128:256, :] = counts.astype(BF)
+        else:
+            wait(in_f.at[pl.ds(0, 127)], h_got.at[it])
+            turned = jnp.swapaxes(in_f[...], 0, 1)
+            for k in range(4):
+                first = jnp.where(core == 0, turned[k], turned[4 + k])
+                second = jnp.where(core == 0, turned[4 + k], turned[k])
+                for apart in range(2):
+                    stack[apart * 128 : apart * 128 + 64, k * 128 : k * 128 + 128] = first[
+                        apart * 64 : apart * 64 + 64
+                    ]
+                    stack[apart * 128 + 64 : apart * 128 + 128, k * 128 : k * 128 + 128] = second[
+                        apart * 64 : apart * 64 + 64
+                    ]
+            total = dot(count_b[...], stack[:, 0:512])
+            for apart in range(2):
+                part = total[apart * 128 : apart * 128 + 128]
+                top = jnp.where(core == 0, part[0:64], part[64:128])
+                low = jnp.where(core == 0, part[64:128], part[0:64])
+                cut = [v[:, k * 128 : k * 128 + 128] for v in (top, low) for k in range(4)]
+                out_f[apart * 64 : apart * 64 + 64] = jnp.swapaxes(jnp.stack(cut, axis=0), 0, 1).astype(BF)
+            send_each(
+                lambda slot, pcore, apart: out_f.at[apart * 64 + slot],
+                lambda apart: got_f.at[me * 2 + core],
+                s_send.at[it], s_got.at[it],
+            )
+            got_f[me * 2 + core] = out_f[me]
         wait(sums_got.at[it, pl.ds(0, 15)], sum_rsem.at[it])
         sums = jnp.sum(sums_got[it], axis=0)
         own_sums = jnp.where(core == 0, sums[4:5, :], sums[5:6, :])
@@ -260,16 +312,23 @@
             for t in range(tiles)
         ]
 
-        wait(got_s.at[it, pl.ds(0, 63)], s_got.at[it])
+        if it == 0:
+            wait(got_s.at[pl.ds(0, 63)], s_got.at[it])
+        else:
+            wait(got_f.at[pl.ds(0, 127)], s_got.at[it])
         news = []
         for t in range(tiles):
-            mat = jnp.concatenate(
-                [
-                    got_s[it, half * 32 : half * 32 + 32].astype(F32)[:, t * 8 : t * 8 + 8, :].reshape(256, 128)
-                    for half in range(2)
-                ],
-                axis=1,
-            ).astype(BF)
+            halves = []
+            for half in range(2):
+                if it == 0:
+                    block = got_s[half * 32 : half * 32 + 32].astype(F32)[:, t * 8 : t * 8 + 8, :]
+                else:
+                    pair = got_f[half * 64 : half * 64 + 64].astype(F32).reshape(32, 2, 8, 128)
+                    block = jnp.where(upper, pair[:, t], pair[:, 1 - t])
+                    if t:
+                        block = pltpu.roll(block, 4, 1)
+                halves.append(block.reshape(256, 128))
+            mat = jnp.concatenate(halves, axis=1).astype(BF)
             form_sum = jnp.sum(
                 esum[t] * dot(mat, cos_b[t]) - ediff[t] * dot(mat, sin_b[t]), axis=0, keepdims=True
             )
@@ -281,13 +340,15 @@
             record = sums_record(estimate)
             rec_send[it + 1] = record
             rec_got[it + 1, row] = record
-            form(it + 1, estimate)
+            cut_by_core(form(estimate))
 
     out_ref[...] = estimate
+    wait(send_h.at[pl.ds(0, 63)], h_send.at[0])
+    wait(other_h, x_send)
+    wait(send_s.at[pl.ds(0, 63)], s_send.at[0])
+    wait(in_f.at[pl.ds(0, 127)], h_send.at[1])
+    wait(out_f.at[pl.ds(0, 127)], s_send.at[1])
     for it in range(ITERS):
-        wait(send_h.at[it, pl.ds(0, 63)], h_send.at[it])
-        wait(other_h.at[it], x_send.at[it])
-        wait(send_s.at[it, pl.ds(0, 63)], s_send.at[it])
         wait(rec_got.at[it, pl.ds(0, 7)], rec_ssem.at[it])
         wait(sums_got.at[it, pl.ds(0, 15)], sum_ssem.at[it])
     wait(count_got.at[pl.ds(0, 240)], cnt_ssem)
@@ -297,7 +358,7 @@
 def on_device(phase, dirty_map, pairs, live):
     tiles, mics, width = phase.shape
     vmem, dma = pltpu.VMEM, pltpu.SemaphoreType.DMA
-    blocks = vmem((ITERS, 64, 16, 128), BF)
+    blocks, fine = vmem((64, 16, 128), BF), vmem((128, 8, 128), BF)
     return pl.pallas_call(
         kernel,
         out_shape=jax.ShapeDtypeStruct(dirty_map.shape, F32),
@@ -314,9 +375,8 @@
             vmem((tiles, mics, width), F32),
             vmem((tiles, mics, width), F32),
             blocks, blocks, blocks, blocks, blocks,
-            vmem((1024, 128), F32),
+            vmem((64, 2, 8, 128), BF), fine, fine, fine,
             vmem((256, 1024), BF),
-            vmem((128, 1024), F32),
             vmem((ITERS, 8, 128), F32),
             vmem((ITERS, 8, 8, 128), F32),
             vmem((ITERS, 8, 128), F32),
@@ -326,10 +386,10 @@
             vmem((16, 256), BF),
             vmem((256, 256), BF),
             vmem((128, 256), F32),
-            vmem((128, 256), BF),
+            vmem((256, 256), BF),
             vmem((256, 256), BF),
             dma((5,)),
-            dma((ITERS,)), dma((ITERS,)), dma((ITERS,)), dma((ITERS,)), dma((ITERS,)), dma((ITERS,)),
+            dma((ITERS,)), dma((ITERS,)), dma, dma, dma((ITERS,)), dma((ITERS,)),
             dma((ITERS,)), dma((ITERS,)), dma((ITERS,)), dma((ITERS,)),
             dma, dma, dma, dma,
         ],

time: 42.9 us -> 42.4 us (0.988)
  Pallas kernels: 41.5 us -> 41 us
    pallas_call x1, Pallas kernels: 41.5 us -> 41 us  [on_device(): pl.pallas_call(kernel, out_shape=jax.ShapeDtypeStruct(dirty_map.shape, F3...]
where the time goes in v4:
time: 42.4 us; the launch traced here: 42.2 us
  Pallas kernels  41 us (97%)
  between operations  0.66 us (2%)
  local copies, waits for them, and re-layouts  0.6 us (1%)
    pallas_call x1, Pallas kernels, on_device(): pl.pallas_call(kernel, out_shape=jax.ShapeDtypeStruct(dirty_map.shape, F3...  41 us

profile of v4, /device:TPU:1, one launch (start us, length us, event | category | flops | bytes accessed | tf_op | source)
XLA Modules:
  0.0 42.2 jit_solution(1002196210503721393)
XLA Ops:
  0.7 41.0 %shard_map.46 = f32[2,512]{1,0:T(2,128)S(1)} custom-call(f32[2,256,512]{2,1,0:T(8,128)} %phase_hbm.1, f32[2,512]{1,0:T(2,128)} %dirty_hbm.1, s32[2,24]{1,0:T(2,128)} %bitcast.1, s32[1]{0:T(128)S(6)} %copy.6.live_hbm), custom_call_target="tpu_custom_call" | custom-call | tf_op jit(solution)/shard_map/pallas_call | solution.py:362
  41.6 0.6 %copy.7 = f32[2,512]{1,0:T(2,128)} copy(f32[2,512]{1,0:T(2,128)S(1)} %shard_map.46) | data formatting | bytes 8192

commit v5 on v4

--- a/solution.py
+++ b/solution.py
@@ -125,18 +125,29 @@
             send_f[pl.ds(half * 32, 32), 0] = jnp.where(upper, first, second).astype(BF)
             send_f[pl.ds(half * 32, 32), 1] = jnp.where(upper, second, first).astype(BF)
 
-    def send_each(src, dst, ssem, rsem):
+    def send_each(src, dst, ssem, rsem, lead=False):
+        targets = []
         for da, db, dc in OFFSETS + [(0, 0, 0)]:
             px = lax.rem(x + da, 4)
             pc = lax.rem(y + db, 4) * 4 + lax.rem(z + dc, 4)
             for apart in range(2):
                 if (da, db, dc) != (0, 0, 0) or apart:
-                    pcore = 1 - core if apart else core
-                    pltpu.make_async_remote_copy(
-                        src_ref=src(pc * 4 + px, pcore, apart), dst_ref=dst(apart),
-                        send_sem=ssem, recv_sem=rsem,
-                        device_id=(px * 2 + pcore, pc), device_id_type=MESH,
-                    ).start()
+                    targets.append((px * 2 + (1 - core if apart else core), pc))
+        if lead:
+            first_row, first_col = targets[0]
+            mine = (row == 1) & (col == 0)
+            moved = [(jnp.where(mine, first_row, 1), jnp.where(mine, first_col, 0))]
+            for prow, pcol in targets[1:]:
+                hit = (prow == 1) & (pcol == 0)
+                moved.append((jnp.where(hit, first_row, prow), jnp.where(hit, first_col, pcol)))
+            targets = moved
+        for prow, pcol in targets:
+            slot, pcore = pcol * 4 + lax.div(prow, 2), lax.rem(prow, 2)
+            apart = lax.rem(core + pcore, 2)
+            pltpu.make_async_remote_copy(
+                src_ref=src(slot, pcore, apart), dst_ref=dst(apart), send_sem=ssem, recv_sem=rsem,
+                device_id=(prow, pcol), device_id_type=MESH,
+            ).start()
 
     def send_all(src, dst, ssem, rsem):
         for da, db, dc in OFFSETS:
@@ -299,7 +310,7 @@
             send_each(
                 lambda slot, pcore, apart: out_f.at[apart * 64 + slot],
                 lambda apart: got_f.at[me * 2 + core],
-                s_send.at[it], s_got.at[it],
+                s_send.at[it], s_got.at[it], lead=True,
             )
             got_f[me * 2 + core] = out_f[me]
         wait(sums_got.at[it, pl.ds(0, 15)], sum_rsem.at[it])

time: 42.4 us -> 41.4 us (0.976)
  Pallas kernels: 41 us -> 39.7 us
    pallas_call x1, Pallas kernels: 41 us -> 39.7 us  [on_device(): pl.pallas_call(kernel, out_shape=jax.ShapeDtypeStruct(dirty_map.shape, F3...]
where the time goes in v5:
time: 41.4 us; the launch traced here: 41 us
  Pallas kernels  39.7 us (96%)
  between operations  0.66 us (2%)
  local copies, waits for them, and re-layouts  0.6 us (1%)
    pallas_call x1, Pallas kernels, on_device(): pl.pallas_call(kernel, out_shape=jax.ShapeDtypeStruct(dirty_map.shape, F3...  39.7 us

profile of v5, /device:TPU:1, one launch (start us, length us, event | category | flops | bytes accessed | tf_op | source)
XLA Modules:
  0.0 41.0 jit_solution(9423460320976077623)
XLA Ops:
  0.7 39.7 %shard_map.46 = f32[2,512]{1,0:T(2,128)S(1)} custom-call(f32[2,256,512]{2,1,0:T(8,128)} %phase_hbm.1, f32[2,512]{1,0:T(2,128)} %dirty_hbm.1, s32[2,24]{1,0:T(2,128)} %bitcast.1, s32[1]{0:T(128)S(6)} %copy.6.live_hbm), custom_call_target="tpu_custom_call" | custom-call | tf_op jit(solution)/shard_map/pallas_call | solution.py:373
  40.4 0.6 %copy.7 = f32[2,512]{1,0:T(2,128)} copy(f32[2,512]{1,0:T(2,128)S(1)} %shard_map.46) | data formatting | bytes 8192

commit v6 on v5

--- a/solution.py
+++ b/solution.py
@@ -8,6 +8,7 @@
 from jax.sharding import PartitionSpec as P
 
 ITERS = 2
+LEAD = (1, 0)
 MESH = pl.DeviceIdType.MESH
 BF = jnp.bfloat16
 F32 = jnp.float32
@@ -133,14 +134,14 @@
             for apart in range(2):
                 if (da, db, dc) != (0, 0, 0) or apart:
                     targets.append((px * 2 + (1 - core if apart else core), pc))
-        if lead:
-            first_row, first_col = targets[0]
-            mine = (row == 1) & (col == 0)
-            moved = [(jnp.where(mine, first_row, 1), jnp.where(mine, first_col, 0))]
-            for prow, pcol in targets[1:]:
-                hit = (prow == 1) & (pcol == 0)
+        for place, ahead in enumerate(LEAD if lead else ()):
+            first_row, first_col = targets[place]
+            mine = (row == ahead) & (col == 0)
+            moved = [(jnp.where(mine, first_row, ahead), jnp.where(mine, first_col, 0))]
+            for prow, pcol in targets[place + 1 :]:
+                hit = (prow == ahead) & (pcol == 0)
                 moved.append((jnp.where(hit, first_row, prow), jnp.where(hit, first_col, pcol)))
-            targets = moved
+            targets = targets[:place] + moved
         for prow, pcol in targets:
             slot, pcore = pcol * 4 + lax.div(prow, 2), lax.rem(prow, 2)
             apart = lax.rem(core + pcore, 2)

time: 41.4 us -> 41.1 us (level)
  no operation moved by 1% of the time
where the time goes in v6:
time: 41.1 us; the launch traced here: 41 us
  Pallas kernels  39.7 us (97%)
  between operations  0.66 us (2%)
  local copies, waits for them, and re-layouts  0.6 us (1%)
    pallas_call x1, Pallas kernels, on_device(): pl.pallas_call(kernel, out_shape=jax.ShapeDtypeStruct(dirty_map.shape, F3...  39.7 us

profile of v6, /device:TPU:1, one launch (start us, length us, event | category | flops | bytes accessed | tf_op | source)
XLA Modules:
  0.0 41.0 jit_solution(12945855922907617665)
XLA Ops:
  0.7 39.7 %shard_map.46 = f32[2,512]{1,0:T(2,128)S(1)} custom-call(f32[2,256,512]{2,1,0:T(8,128)} %phase_hbm.1, f32[2,512]{1,0:T(2,128)} %dirty_hbm.1, s32[2,24]{1,0:T(2,128)} %bitcast.1, s32[1]{0:T(128)S(6)} %copy.6.live_hbm), custom_call_target="tpu_custom_call" | custom-call | tf_op jit(solution)/shard_map/pallas_call | solution.py:374
  40.4 0.6 %copy.7 = f32[2,512]{1,0:T(2,128)} copy(f32[2,512]{1,0:T(2,128)S(1)} %shard_map.46) | data formatting | bytes 8192

commit v7 on v6

--- a/solution.py
+++ b/solution.py
@@ -24,7 +24,10 @@
 
 OFFSETS = sorted(
     [(a, b, c) for a in range(4) for b in range(4) for c in range(4) if (a, b, c) != (0, 0, 0)],
-    key=lambda offset: -hops(offset),
+    key=lambda offset: (-hops(offset), offset.count(2)),
+)
+OFFSETS = list(
+    dict.fromkeys(o for offset in OFFSETS for o in (offset, tuple(-step % 4 for step in offset)))
 )
 
 
@@ -254,6 +257,9 @@
                 lambda apart: in_f.at[apart * 64 + me],
                 h_send.at[it], h_got.at[it],
             )
+            record = sums_record(estimate)
+            rec_send[it] = record
+            rec_got[it, row] = record
             send_row(rec_send.at[it], rec_got.at[it], rec_ssem.at[it], rec_rsem.at[it])
             in_f[me] = send_f[me, core]
 
@@ -349,9 +355,6 @@
             news.append(jnp.maximum(old + (dirty[t : t + 1, :] - value) / diag[t : t + 1], 0.0))
         estimate = jnp.concatenate(news, axis=0)
         if it + 1 < ITERS:
-            record = sums_record(estimate)
-            rec_send[it + 1] = record
-            rec_got[it + 1, row] = record
             cut_by_core(form(estimate))
 
     out_ref[...] = estimate

time: 41.1 us -> 40.6 us (0.988)
  Pallas kernels: 39.7 us -> 39.2 us
    pallas_call x1, Pallas kernels: 39.7 us -> 39.2 us  [on_device(): pl.pallas_call(kernel, out_shape=jax.ShapeDtypeStruct(dirty_map.shape, F3...]
where the time goes in v7:
time: 40.6 us; the launch traced here: 40.4 us
  Pallas kernels  39.2 us (97%)
  between operations  0.66 us (2%)
  local copies, waits for them, and re-layouts  0.6 us (1%)
    pallas_call x1, Pallas kernels, on_device(): pl.pallas_call(kernel, out_shape=jax.ShapeDtypeStruct(dirty_map.shape, F3...  39.2 us

profile of v7, /device:TPU:1, one launch (start us, length us, event | category | flops | bytes accessed | tf_op | source)
XLA Modules:
  0.0 40.4 jit_solution(4721379555930573340)
XLA Ops:
  0.7 39.2 %shard_map.46 = f32[2,512]{1,0:T(2,128)S(1)} custom-call(f32[2,256,512]{2,1,0:T(8,128)} %phase_hbm.1, f32[2,512]{1,0:T(2,128)} %dirty_hbm.1, s32[2,24]{1,0:T(2,128)} %bitcast.1, s32[1]{0:T(128)S(6)} %copy.6.live_hbm), custom_call_target="tpu_custom_call" | custom-call | tf_op jit(solution)/shard_map/pallas_call | solution.py:377
  39.8 0.6 %copy.7 = f32[2,512]{1,0:T(2,128)} copy(f32[2,512]{1,0:T(2,128)S(1)} %shard_map.46) | data formatting | bytes 8192

commit v8 on v7

--- a/solution.py
+++ b/solution.py
@@ -129,7 +129,7 @@
             send_f[pl.ds(half * 32, 32), 0] = jnp.where(upper, first, second).astype(BF)
             send_f[pl.ds(half * 32, 32), 1] = jnp.where(upper, second, first).astype(BF)
 
-    def send_each(src, dst, ssem, rsem, lead=False):
+    def send_each(src, dst, ssem, rsem, lead=False, midway=None):
         targets = []
         for da, db, dc in OFFSETS + [(0, 0, 0)]:
             px = lax.rem(x + da, 4)
@@ -145,7 +145,9 @@
                 hit = (prow == ahead) & (pcol == 0)
                 moved.append((jnp.where(hit, first_row, prow), jnp.where(hit, first_col, pcol)))
             targets = targets[:place] + moved
-        for prow, pcol in targets:
+        for place, (prow, pcol) in enumerate(targets):
+            if midway is not None and place == 64:
+                midway()
             slot, pcore = pcol * 4 + lax.div(prow, 2), lax.rem(prow, 2)
             apart = lax.rem(core + pcore, 2)
             pltpu.make_async_remote_copy(
@@ -252,15 +254,17 @@
             )
             exchange.start()
         else:
+            def send_sums():
+                record = sums_record(estimate)
+                rec_send[it] = record
+                rec_got[it, row] = record
+                send_row(rec_send.at[it], rec_got.at[it], rec_ssem.at[it], rec_rsem.at[it])
+
             send_each(
                 lambda slot, pcore, apart: send_f.at[slot, pcore],
                 lambda apart: in_f.at[apart * 64 + me],
-                h_send.at[it], h_got.at[it],
+                h_send.at[it], h_got.at[it], midway=send_sums,
             )
-            record = sums_record(estimate)
-            rec_send[it] = record
-            rec_got[it, row] = record
-            send_row(rec_send.at[it], rec_got.at[it], rec_ssem.at[it], rec_rsem.at[it])
             in_f[me] = send_f[me, core]
 
         wait(rec_got.at[it, pl.ds(0, 7)], rec_rsem.at[it])

time: 40.6 us -> 40.6 us (level)
  no operation moved by 1% of the time
where the time goes in v8:
time: 40.6 us; the launch traced here: 40.4 us
  Pallas kernels  39.2 us (97%)
  between operations  0.66 us (2%)
  local copies, waits for them, and re-layouts  0.6 us (1%)
    pallas_call x1, Pallas kernels, on_device(): pl.pallas_call(kernel, out_shape=jax.ShapeDtypeStruct(dirty_map.shape, F3...  39.2 us

profile of v8, /device:TPU:1, one launch (start us, length us, event | category | flops | bytes accessed | tf_op | source)
XLA Modules:
  0.0 40.4 jit_solution(1231880639757322828)
XLA Ops:
  0.7 39.2 %shard_map.46 = f32[2,512]{1,0:T(2,128)S(1)} custom-call(f32[2,256,512]{2,1,0:T(8,128)} %phase_hbm.1, f32[2,512]{1,0:T(2,128)} %dirty_hbm.1, s32[2,24]{1,0:T(2,128)} %bitcast.1, s32[1]{0:T(128)S(6)} %copy.6.live_hbm), custom_call_target="tpu_custom_call" | custom-call | tf_op jit(solution)/shard_map/pallas_call | solution.py:381
  39.8 0.6 %copy.7 = f32[2,512]{1,0:T(2,128)} copy(f32[2,512]{1,0:T(2,128)S(1)} %shard_map.46) | data formatting | bytes 8192

commit v9 on v8

--- a/solution.py
+++ b/solution.py
@@ -24,7 +24,7 @@
 
 OFFSETS = sorted(
     [(a, b, c) for a in range(4) for b in range(4) for c in range(4) if (a, b, c) != (0, 0, 0)],
-    key=lambda offset: (-hops(offset), offset.count(2)),
+    key=lambda offset: (-hops(offset), offset.count(2), offset[0] == 2),
 )
 OFFSETS = list(
     dict.fromkeys(o for offset in OFFSETS for o in (offset, tuple(-step % 4 for step in offset)))

time: 40.6 us -> 40.6 us (level)
  no operation moved by 1% of the time
where the time goes in v9:
time: 40.6 us; the launch traced here: 40.4 us
  Pallas kernels  39.2 us (97%)
  between operations  0.66 us (2%)
  local copies, waits for them, and re-layouts  0.6 us (1%)
    pallas_call x1, Pallas kernels, on_device(): pl.pallas_call(kernel, out_shape=jax.ShapeDtypeStruct(dirty_map.shape, F3...  39.2 us

profile of v9, /device:TPU:1, one launch (start us, length us, event | category | flops | bytes accessed | tf_op | source)
XLA Modules:
  0.0 40.4 jit_solution(1231880639757322828)
XLA Ops:
  0.7 39.2 %shard_map.46 = f32[2,512]{1,0:T(2,128)S(1)} custom-call(f32[2,256,512]{2,1,0:T(8,128)} %phase_hbm.1, f32[2,512]{1,0:T(2,128)} %dirty_hbm.1, s32[2,24]{1,0:T(2,128)} %bitcast.1, s32[1]{0:T(128)S(6)} %copy.6.live_hbm), custom_call_target="tpu_custom_call" | custom-call | tf_op jit(solution)/shard_map/pallas_call | solution.py:381
  39.8 0.6 %copy.7 = f32[2,512]{1,0:T(2,128)} copy(f32[2,512]{1,0:T(2,128)S(1)} %shard_map.46) | data formatting | bytes 8192
